TPU v7x, 32 devices: a whole 2x2x4 slice. The times are simulated.
32 devices in a mesh: seq: 8 (over y, x, core), head: 4 (over z).
Axes of the slice: x: 2, y: 2, z: 4, core: 2. Of those that a mesh axis runs over, the one named last changes fastest.
Arguments:
- q_rows: float32 [2048, 2048], P(('seq', 'head')), may hold values from -4 to 4
- k_rows: float32 [2048, 2048], P(('seq', 'head')), may hold values from -4 to 4
- v_rows: float32 [2048, 2048], P(('seq', 'head')), may hold values from -6 to 6
- step_sizes: float32 [8, 2048], P('head', 'seq'), may hold values from 0.1 to 1
- fast_weights: float32 [3, 8, 256, 512], P(None, 'head'), may hold values from -0.375 to 0.375
- norm_gain: float32 [2048], P('head'), may hold values from 0.1 to 1.9
- w_out: bfloat16 [2048, 4096], P('head'), may hold values from -0.125 to 0.125
Outputs:
- mixed_out: bfloat16 [2048, 4096], P(('seq', 'head'))
- new_weights: float32 [3, 8, 256, 512], P(None, 'head')
All inputs are finite; a program needn't handle non-finite values.
Results may differ from a plain program's by a relative error of at most 0.005.
Values sent between devices are 32-bit elements; how exact they have to be, the bound alone decides.
A program may use at most 128 MiB of HBM per device.

v0:
```python
import functools
import math

import jax
import jax.numpy as jnp
from jax import lax
from jax.experimental import pallas as pl
from jax.experimental.pallas import tpu as pltpu
from jax.sharding import PartitionSpec as P

WINDOW = 256
NS_ITERS = 3

epsilon = 1e-06
coef_linear = 3.4445
coef_square = -4.775
coef_cubic = 2.0315

MESH = pl.DeviceIdType.MESH
f32, bf16 = jnp.float32, jnp.bfloat16


def dot(a, b, dims=((1,), (0,))):
    return lax.dot_general(
        a.astype(bf16), b.astype(bf16), (dims, ((), ())), preferred_element_type=f32
    )


NT, TN = ((1,), (1,)), ((0,), (0,))


def split(x):
    high = x.astype(bf16)
    return high, (x - high.astype(f32)).astype(bf16)


def dot3(a, b, dims=((1,), (0,))):
    a_high, a_low = a if isinstance(a, tuple) else split(a)
    b_high, b_low = b if isinstance(b, tuple) else split(b)
    small = dot(a_high, b_low, dims) + dot(a_low, b_high, dims)
    return dot(a_high, b_high, dims) + small


def kernel(
    ns, nz, chunks,
    q_in, k_in, v_in, step_ref, fw_in, gain_ref, w_in,
    out_ref, new_ref,
    qkv, halo, fw, w_out, grads, swap, rs_in, full, new, comb, part, up, down,
    a2a_send, a2a_recv, own_sem, halo_send, halo_recv, load_sem,
    swap_send, swap_recv, rs_send, rs_recv, ag_send, ag_recv,
    new_send, new_recv, store_sem, up_send, up_recv, down_send, down_recv,
):
    s, z = lax.axis_index("seq"), lax.axis_index("head")
    length, width = qkv.shape[1], qkv.shape[2]
    rows = length // nz
    head_dim, hidden = fw.shape[2], fw.shape[3]
    bits = ns.bit_length() - 1
    core = lax.rem(s, 2)

    def bit_of(bit):
        return lax.rem(s // (1 << bit), 2)

    def across(bit):
        return s + (1 - 2 * bit_of(bit)) * (1 << bit)

    def at(seq, head):
        return (seq, head)

    later, earlier = lax.rem(s + 1, ns), lax.rem(s + ns - 1, ns)
    loads = [
        pltpu.make_async_copy(fw_in, fw, load_sem.at[0]),
        pltpu.make_async_copy(w_in, w_out, load_sem.at[1]),
    ]
    loads[0].start()
    own = []
    for array, source in ((1, k_in), (2, v_in), (0, q_in)):
        copy = pltpu.make_async_copy(
            source.at[:, pl.ds(pl.multiple_of(z * width, width), width)],
            qkv.at[array, pl.ds(pl.multiple_of(z * rows, rows), rows)],
            own_sem.at[array],
        )
        copy.start()
        own.append(copy)

    barrier = pltpu.get_barrier_semaphore()
    partners = [at(s, lax.rem(z + off, nz)) for off in range(1, nz)]
    partners += [at(across(bit), z) for bit in range(bits)]
    partners += [at(later, z), at(earlier, z)]
    for partner in partners:
        pl.semaphore_signal(barrier, inc=1, device_id=partner, device_id_type=MESH)
    pl.semaphore_wait(barrier, len(partners))

    a2a = {}

    def exchange(array, source):
        for off in range(1, nz):
            target = lax.rem(z + off, nz)
            copy = pltpu.make_async_remote_copy(
                source.at[:, pl.ds(pl.multiple_of(target * width, width), width)],
                qkv.at[array, pl.ds(pl.multiple_of(z * rows, rows), rows)],
                a2a_send.at[array, off - 1],
                a2a_recv.at[array, off - 1],
                device_id=at(s, target),
                device_id_type=MESH,
            )
            copy.start()
            a2a[array, off] = copy

    exchange(1, k_in)
    exchange(2, v_in)
    loads[1].start()

    def arrived(array):
        for off in range(1, nz):
            a2a[array, off].wait_recv()

    halos = []

    def send_halo(which):
        copy = pltpu.make_async_remote_copy(
            qkv.at[which + 1], halo.at[which], halo_send.at[which], halo_recv.at[which],
            device_id=at(later, z), device_id_type=MESH,
        )
        copy.start()
        halos.append(copy)

    own[0].wait()
    arrived(1)
    send_halo(0)
    loads[0].wait()
    head_cols = lambda h: pl.ds(pl.multiple_of(h * head_dim, head_dim), head_dim)

    other = 1 - core
    forward = []
    for h in (other, core):
        key = split(qkv[1, :, head_cols(h)])
        gate = dot3(key, fw[0, h])
        up_pre = dot3(key, fw[2, h])
        sig = jax.nn.sigmoid(gate)
        active = gate * sig
        glu = active * up_pre
        slope = up_pre * sig * (1.0 + gate * (1.0 - sig))
        forward.append((h, key, active, glu, slope))
    own[1].wait()
    arrived(2)
    send_halo(1)
    exchange(0, q_in)
    swaps = []
    for turn, (h, key, active, glu, slope) in enumerate(forward):
        upstream = split(-(qkv[2, :, head_cols(h)].T) * step_ref[pl.ds(h, 1), :])
        back = dot3(upstream, fw[1, h], TN)
        for m, value in (
            (1, lambda: dot3(upstream, glu)),
            (2, lambda: dot3(key, back * active, TN)),
            (0, lambda: dot3(key, back * slope, TN)),
        ):
            grads[turn, pl.ds(m * head_dim, head_dim)] = value()
            if turn == 0:
                copy = pltpu.make_async_remote_copy(
                    grads.at[0, pl.ds(m * head_dim, head_dim)],
                    swap.at[pl.ds(m * head_dim, head_dim)],
                    swap_send.at[m], swap_recv.at[m],
                    device_id=at(across(0), z), device_id_type=MESH,
                )
                copy.start()
                swaps.append((m, copy))
    for m, copy in swaps:
        copy.wait()
        block = pl.ds(m * head_dim, head_dim)
        grads[1, block] = grads[1, block] + swap[block]

    total_rows = 3 * head_dim
    half_cols = hidden // 2
    orders = [list(range(1, bits)), list(range(bits - 1, 0, -1))]
    lo = [0, 0]
    spans = [[], []]
    size, base = total_rows, 0

    def attend(h):
        query = qkv[0, :, head_cols(h)]
        scores = jnp.concatenate(
            [
                dot(query, halo[0, :, head_cols(h)], NT),
                dot(query, qkv[1, :, head_cols(h)], NT),
            ],
            axis=1,
        ) * (1.0 / math.sqrt(head_dim))
        query_pos = lax.broadcasted_iota(jnp.int32, scores.shape, 0)
        key_pos = lax.broadcasted_iota(jnp.int32, scores.shape, 1) - length
        allowed = (
            (key_pos <= query_pos) & (key_pos > query_pos - WINDOW) & (key_pos >= -s * length)
        )
        scores = jnp.where(allowed, scores, -1e30)
        expo = jnp.exp(scores - jnp.max(scores, axis=-1, keepdims=True))
        weights = expo / jnp.sum(expo, axis=-1, keepdims=True)
        return dot(weights[:, :length], halo[1, :, head_cols(h)]) + dot(
            weights[:, length:], qkv[2, :, head_cols(h)]
        )

    attended = []

    def attention():
        own[2].wait()
        arrived(0)
        for copy in halos:
            copy.wait()
        for h in (core, other):
            attended.append(attend(h))

    for step in range(bits - 1):
        size //= 2
        pending = []
        for side in range(2):
            bit = orders[side][step]
            mine = bit_of(bit)
            cols = pl.ds(side * half_cols, half_cols)
            give = pl.multiple_of(lo[side] + (1 - mine) * size, 8)
            copy = pltpu.make_async_remote_copy(
                grads.at[1, pl.ds(give, size), cols],
                rs_in.at[pl.ds(base, size), cols],
                rs_send.at[side, step], rs_recv.at[side, step],
                device_id=at(across(bit), z), device_id_type=MESH,
            )
            copy.start()
            pending.append(copy)
            spans[side].append((lo[side], lo[side] + mine * size, size, bit))
            lo[side] = lo[side] + mine * size
        if step == min(1, bits - 2):
            attention()
        for side in range(2):
            pending[side].wait()
            cols = pl.ds(side * half_cols, half_cols)
            keep = pl.ds(pl.multiple_of(lo[side], 8), size)
            total = grads[1, keep, cols] + rs_in[pl.ds(base, size), cols]
            if step == bits - 2:
                full[keep, cols] = total
            else:
                grads[1, keep, cols] = total
        base += size
    for step in range(bits - 2, -1, -1):
        pending = []
        for side in range(2):
            _, start, size, bit = spans[side][step]
            block = full.at[
                pl.ds(pl.multiple_of(start, 8), size), pl.ds(side * half_cols, half_cols)
            ]
            copy = pltpu.make_async_remote_copy(
                block, block, ag_send.at[side, step], ag_recv.at[side, step],
                device_id=at(across(bit), z), device_id_type=MESH,
            )
            copy.start()
            pending.append(copy)
        for copy in pending:
            copy.wait()

    mats = []
    for m in range(3):
        g = full[pl.ds(m * head_dim, head_dim)]
        mats.append(g * (1.0 / (jnp.sqrt(jnp.sum(g * g)) + epsilon)))
    for _ in range(NS_ITERS):
        pairs = [split(x) for x in mats]
        grams = [dot3(x, x, NT) for x in pairs]
        squares = [split(a) for a in grams]
        polys = [coef_square * a + coef_cubic * dot3(b, b) for a, b in zip(grams, squares)]
        mats = [coef_linear * x + dot3(p, y) for p, x, y in zip(polys, mats, pairs)]
    news = []
    stores = []
    for m in (0, 2, 1):
        old = fw[m, core]
        cand = old - mats[m]
        target = jnp.sqrt(jnp.sum(old * old, axis=0, keepdims=True))
        current = jnp.sqrt(jnp.sum(cand * cand, axis=0, keepdims=True)) + epsilon
        new[m, core] = cand * (target / current)
        copy = pltpu.make_async_remote_copy(
            new.at[m, core], new.at[m, core], new_send.at[m], new_recv.at[m],
            device_id=at(across(0), z), device_id_type=MESH,
        )
        copy.start()
        news.append(copy)
        copy = pltpu.make_async_copy(new.at[m, core], new_ref.at[m, core], store_sem.at[0, m])
        copy.start()
        stores.append(copy)

    def mix(h, attended_h):
        query = split(qkv[0, :, head_cols(h)])
        gate = dot3(query, new[0, h])
        up_pre = dot3(query, new[2, h])
        fast = dot3(gate * jax.nn.sigmoid(gate) * up_pre, new[1, h], NT)
        fast = fast * lax.rsqrt(jnp.mean(fast * fast, axis=-1, keepdims=True) + epsilon)
        fast = fast * gain_ref[:, head_cols(h)]
        comb[:, head_cols(h)] = (fast + attended_h).astype(bf16)

    mix(core, attended[0])
    for copy in news:
        copy.wait()
    for m in range(3):
        copy = pltpu.make_async_copy(new.at[m, other], new_ref.at[m, other], store_sem.at[1, m])
        copy.start()
        stores.append(copy)
    mix(other, attended[1])

    loads[1].wait()
    columns = w_out.shape[1]
    wide = columns // chunks
    above, below = lax.rem(z + 1, nz), lax.rem(z + nz - 1, nz)

    def flow(d, q, upward):
        cols = pl.ds(q * wide, wide)
        landing, send, recv = (up, up_send, up_recv) if upward else (down, down_send, down_recv)
        return pltpu.make_async_remote_copy(
            part.at[d, :, cols], landing.at[d, :, cols], send.at[d, q], recv.at[d, q],
            device_id=at(s, above if upward else below), device_id_type=MESH,
        )

    def moves(d, upward):
        return (z < d) if upward else (z > d)

    def comes(d, upward):
        return ((z > 0) & (z <= d)) if upward else ((z < nz - 1) & (z >= d))

    order = []
    for i in range(nz):
        order += [(nz - 1 - i, True), (i, False)]

    for q in range(chunks):
        cols = pl.ds(q * wide, wide)
        whole = dot(comb[...], w_out[:, cols])
        for d in range(nz):
            part[d, :, cols] = whole[d * rows : (d + 1) * rows]
        for d, upward in order:
            first = (z == 0) if upward else (z == nz - 1)

            @pl.when(first & moves(d, upward))
            def _():
                flow(d, q, upward).start()

    for q in range(chunks):
        cols = pl.ds(q * wide, wide)
        for d, upward in order:
            landing = up if upward else down

            @pl.when(comes(d, upward))
            def _():
                flow(d, q, upward).wait_recv()
                part[d, :, cols] = part[d, :, cols] + landing[d, :, cols]

                @pl.when(moves(d, upward))
                def _():
                    flow(d, q, upward).start()

        out_ref[:, cols] = part[z, :, cols].astype(out_ref.dtype)

    for q in range(chunks):
        for d, upward in order:

            @pl.when(moves(d, upward))
            def _():
                flow(d, q, upward).wait_send()

    for copy in stores:
        copy.wait()
    for copy in a2a.values():
        copy.wait_send()


def solution(mesh):
    ns, nz = mesh.shape["seq"], mesh.shape["head"]
    chunks = 4

    def local(q_rows, k_rows, v_rows, step_sizes, fast_weights, norm_gain, w_out):
        mats, heads, head_dim, hidden = fast_weights.shape
        width, length = heads * head_dim, q_rows.shape[0] * nz
        rows, columns = q_rows.shape[0], w_out.shape[1]
        bits = ns.bit_length() - 1
        dma = pltpu.SemaphoreType.DMA
        anywhere = pl.BlockSpec(memory_space=pl.ANY)
        vmem = pl.BlockSpec(memory_space=pltpu.VMEM)
        return pl.pallas_call(
            functools.partial(kernel, ns, nz, chunks),
            out_shape=(
                jax.ShapeDtypeStruct((rows, columns), bf16),
                jax.ShapeDtypeStruct(fast_weights.shape, f32),
            ),
            in_specs=[anywhere, anywhere, anywhere, vmem, anywhere, vmem, anywhere],
            out_specs=(vmem, anywhere),
            scratch_shapes=[
                pltpu.VMEM((3, length, width), f32),
                pltpu.VMEM((2, length, width), f32),
                pltpu.VMEM(fast_weights.shape, f32),
                pltpu.VMEM(w_out.shape, w_out.dtype),
                pltpu.VMEM((2, mats * head_dim, hidden), f32),
                pltpu.VMEM((mats * head_dim, hidden), f32),
                pltpu.VMEM((mats * head_dim, hidden), f32),
                pltpu.VMEM((mats * head_dim, hidden), f32),
                pltpu.VMEM(fast_weights.shape, f32),
                pltpu.VMEM((length, width), bf16),
                pltpu.VMEM((nz, rows, columns), f32),
                pltpu.VMEM((nz, rows, columns), f32),
                pltpu.VMEM((nz, rows, columns), f32),
                dma((3, nz - 1)), dma((3, nz - 1)), dma((3,)), dma((2,)), dma((2,)), dma((2,)),
                dma((3,)), dma((3,)),
                dma((2, bits - 1)), dma((2, bits - 1)), dma((2, bits - 1)), dma((2, bits - 1)),
                dma((3,)), dma((3,)), dma((2, 3)),
                dma((nz, chunks)), dma((nz, chunks)), dma((nz, chunks)), dma((nz, chunks)),
            ],
            compiler_params=pltpu.CompilerParams(
                collective_id=0, has_side_effects=True, vmem_limit_bytes=56 * 2**20
            ),
        )(
            q_rows, k_rows, v_rows, step_sizes, fast_weights,
            norm_gain.reshape(1, -1), w_out,
        )

    return jax.shard_map(
        local,
        mesh=mesh,
        in_specs=(
            P(("seq", "head"), None),
            P(("seq", "head"), None),
            P(("seq", "head"), None),
            P("head", "seq"),
            P(None, "head", None, None),
            P("head"),
            P("head", None),
        ),
        out_specs=(P(("seq", "head"), None), P(None, "head", None, None)),
        check_vma=False,
    )
```

profile of v0, /device:TPU:8, one launch (start us, length us, event | category | flops | bytes accessed | tf_op | source)
XLA Modules:
  0.0 185.1 jit_solution(8597924500205719872)
XLA Ops:
  0.6 178.5 %shard_map.86 = (bf16[64,4096]{1,0:T(8,128)(2,1)}, f32[3,2,256,512]{3,2,1,0:T(8,128)}) custom-call(f32[64,2048]{1,0:T(8,128)} %q_in.1, f32[64,2048]{1,0:T(8,128)} %k_in.1, f32[64,2048]{1,0:T(8,128)} %v_in.1, f32[2,256]{1,0:T(2,128)} %step_ref.1, f32[3,2,256,512]{3,2,1,0:T(8,128)} %fw_in.1, f32[1,512]{1,0:T(1,128)} %bitcast.1, bf16[512,4096]{1,0:T(8,128)(2,1)} %w_in.1), custom_call_target="tpu_custom_call" | custom-call | tf_op jit(solution)/shard_map/pallas_call | solution.py:378
  179.1 1.9 %copy.11 = bf16[64,4096]{1,0:T(8,128)(2,1)} copy(bf16[64,4096]{1,0:T(8,128)(2,1)} %get-tuple-element.4) | data formatting | bytes 1048576
  181.0 4.1 %copy.12 = f32[3,2,256,512]{3,2,1,0:T(8,128)} copy(f32[3,2,256,512]{3,2,1,0:T(8,128)} %get-tuple-element.5) | data formatting | bytes 6291456
where the time goes:
time: 185 us
  Pallas kernels  179 us (97%)
  local copies, waits for them, and re-layouts  6 us (3%)
    pallas_call x1, Pallas kernels, local(): pl.pallas_call(functools.partial(kernel, ns, nz, chunks), out_shape=(jax....  179 us
    unnamed x2, local copies, waits for them, and re-layouts  6 us

commit v1 on v0

--- a/solution.py
+++ b/solution.py
@@ -305,7 +305,7 @@
     above, below = lax.rem(z + 1, nz), lax.rem(z + nz - 1, nz)
 
     def flow(d, q, upward):
-        cols = pl.ds(q * wide, wide)
+        cols = pl.ds(pl.multiple_of(q * wide, wide), wide)
         landing, send, recv = (up, up_send, up_recv) if upward else (down, down_send, down_recv)
         return pltpu.make_async_remote_copy(
             part.at[d, :, cols], landing.at[d, :, cols], send.at[d, q], recv.at[d, q],
@@ -322,8 +322,9 @@
     for i in range(nz):
         order += [(nz - 1 - i, True), (i, False)]
 
-    for q in range(chunks):
-        cols = pl.ds(q * wide, wide)
+    @pl.loop(0, chunks)
+    def _(q):
+        cols = pl.ds(pl.multiple_of(q * wide, wide), wide)
         whole = dot(comb[...], w_out[:, cols])
         for d in range(nz):
             part[d, :, cols] = whole[d * rows : (d + 1) * rows]
@@ -334,8 +335,9 @@
             def _():
                 flow(d, q, upward).start()
 
-    for q in range(chunks):
-        cols = pl.ds(q * wide, wide)
+    @pl.loop(0, chunks)
+    def _(q):
+        cols = pl.ds(pl.multiple_of(q * wide, wide), wide)
         for d, upward in order:
             landing = up if upward else down
 
@@ -350,7 +352,8 @@
 
         out_ref[:, cols] = part[z, :, cols].astype(out_ref.dtype)
 
-    for q in range(chunks):
+    @pl.loop(0, chunks)
+    def _(q):
         for d, upward in order:
 
             @pl.when(moves(d, upward))
@@ -365,7 +368,7 @@
 
 def solution(mesh):
     ns, nz = mesh.shape["seq"], mesh.shape["head"]
-    chunks = 4
+    chunks = 8
 
     def local(q_rows, k_rows, v_rows, step_sizes, fast_weights, norm_gain, w_out):
         mats, heads, head_dim, hidden = fast_weights.shape

time: 185 us -> 223 us (1.21)
  Pallas kernels: 179 us -> 216 us
    pallas_call x1, Pallas kernels: 179 us -> 216 us  [local(): pl.pallas_call(functools.partial(kernel, ns, nz, chunks), out_shape=(jax....]
where the time goes in v1:
time: 223 us
  Pallas kernels  216 us (97%)
  local copies, waits for them, and re-layouts  6 us (3%)
    pallas_call x1, Pallas kernels, local(): pl.pallas_call(functools.partial(kernel, ns, nz, chunks), out_shape=(jax....  216 us
    unnamed x2, local copies, waits for them, and re-layouts  6 us

profile of v1, /device:TPU:8, one launch (start us, length us, event | category | flops | bytes accessed | tf_op | source)
XLA Modules:
  0.0 222.8 jit_solution(5974688531951886359)
XLA Ops:
  0.6 216.1 %shard_map.86 = (bf16[64,4096]{1,0:T(8,128)(2,1)}, f32[3,2,256,512]{3,2,1,0:T(8,128)}) custom-call(f32[64,2048]{1,0:T(8,128)} %q_in.1, f32[64,2048]{1,0:T(8,128)} %k_in.1, f32[64,2048]{1,0:T(8,128)} %v_in.1, f32[2,256]{1,0:T(2,128)} %step_ref.1, f32[3,2,256,512]{3,2,1,0:T(8,128)} %fw_in.1, f32[1,512]{1,0:T(1,128)} %bitcast.1, bf16[512,4096]{1,0:T(8,128)(2,1)} %w_in.1), custom_call_target="tpu_custom_call" | custom-call | tf_op jit(solution)/shard_map/pallas_call | solution.py:381
  216.8 1.9 copy.11
  218.6 4.1 %copy.12 = f32[3,2,256,512]{3,2,1,0:T(8,128)} copy(f32[3,2,256,512]{3,2,1,0:T(8,128)} %get-tuple-element.5) | data formatting | bytes 6291456
